TPU v7x, 128 devices: a whole 4x4x4 slice. The times are simulated.
128 devices in a mesh: sub: 32 (over z_lo, x, y), col: 4 (over z_hi, core).
Axes of the slice: x: 4, y: 4, z: 4 (z_hi: 2, z_lo: 2; z = z_hi * 2 + z_lo), core: 2. Of those that a mesh axis runs over, the one named last changes fastest.
Arguments:
- loads: float32 [32, 8, 1024, 256], P('sub', 'col')
- schur: float32 [32, 8, 1024, 1024], P('sub', 'col')
- local_inv: float32 [32, 8, 1024, 1024], P('sub', 'col')
- basis: float32 [32, 8, 48, 1024], P('sub', 'col'), may hold values from -0.5 to 0.5
- coarse_inv: float32 [32, 192, 192], P('sub')
- primal: int32 [32, 8, 48], P('sub', 'col'), may hold values from 0 to 191
- block_roles: int32 [32, 8, 8], P('sub', 'col'), may hold values from 0 to 7, each once within a row
Outputs:
- solution: float32 [32, 8, 1024, 256], P('sub', 'col')
- residual: float32 [32, 8, 1024, 256], P('sub', 'col')
All inputs are finite; a program needn't handle non-finite values.
Results may differ from a plain program's by a relative error of at most 0.00023.
Values sent between devices are 32-bit elements; how exact they have to be, the bound alone decides.
A program may use at most 128 MiB of HBM per device.

v0:
```python
import jax
import jax.numpy as jnp
from jax import lax
from jax.sharding import PartitionSpec as P

NB = 8
BLOCK = 128
ITERS = 2


HIGH = lax.Precision.HIGHEST


def from_behind(value, axis, steps):
    count = lax.axis_size(axis)
    pairs = [(source, (source + steps) % count) for source in range(count)]
    return lax.ppermute(value, axis, pairs)


def neighbour_sum(vector, table):
    lead = vector.shape
    blocks = vector.reshape(lead[0], lead[1], NB, BLOCK, lead[3])
    by_role = jnp.einsum("rcks,rcsbn->rckbn", table, blocks, precision=HIGH)
    pack_down = jnp.concatenate([by_role[:, :, 2:4], by_role[:, ::-1, 7:8]], axis=2)
    pack_up = jnp.concatenate([by_role[:, :, 0:2], by_role[:, ::-1, 6:7]], axis=2)
    from_prior = from_behind(pack_down, "sub", 1)
    from_next = from_behind(pack_up, "sub", -1)
    received = jnp.concatenate(
        [
            from_prior[:, :, 0:2],
            from_next[:, :, 0:2],
            by_role[:, ::-1, 4:6],
            from_prior[:, :, 2:3],
            from_next[:, :, 2:3],
        ],
        axis=2,
    )
    back = jnp.einsum("rcks,rckbn->rcsbn", table, received, precision=HIGH)
    return vector + back.reshape(lead)


def apply_schur(direction, schur, table):
    return neighbour_sum(jnp.einsum("rcij,rcjn->rcin", schur, direction, precision=HIGH), table)


def precondition(vector, basis, local_inv, onehot, coarse_inv, table):
    weighted = 0.5 * vector
    rows = jnp.einsum("rcpi,rcin->rcpn", basis, weighted, precision=HIGH)
    own = jnp.einsum("rcpg,rcpn->gn", onehot, rows, precision=HIGH)
    assembled = lax.psum(own, "col")
    coarse = jnp.dot(coarse_inv[0], assembled, precision=HIGH)
    spread = jnp.einsum("rcpg,gn->rcpn", onehot, coarse, precision=HIGH)
    local = jnp.einsum("rcij,rcjn->rcin", local_inv, weighted, precision=HIGH)
    local = local + jnp.einsum("rcpi,rcpn->rcin", basis, spread, precision=HIGH)
    return 0.5 * neighbour_sum(local, table)


def partial_inner(left, right):
    return 0.5 * jnp.sum(left * right, axis=(0, 1, 2))


def residual_product(residual, precond):
    return lax.psum(partial_inner(residual, precond), ("sub", "col"))


def curvature_product(direction, image):
    return lax.psum(partial_inner(direction, image), ("sub", "col"))


def body(loads, schur, local_inv, basis, coarse_inv, primal, block_roles):
    count_coarse = coarse_inv.shape[-1]
    table = (block_roles[..., None] == jnp.arange(NB, dtype=jnp.int32)).astype(jnp.float32)
    onehot = (primal[..., None] == jnp.arange(count_coarse, dtype=jnp.int32)).astype(jnp.float32)
    residual = neighbour_sum(loads, table)
    solution = jnp.zeros_like(residual)
    precond = precondition(residual, basis, local_inv, onehot, coarse_inv, table)
    direction = precond
    rz_now = residual_product(residual, precond)
    for step in range(ITERS):
        image = apply_schur(direction, schur, table)
        alpha = rz_now / curvature_product(direction, image)
        solution = solution + alpha * direction
        residual = residual - alpha * image
        if step + 1 < ITERS:
            precond = precondition(residual, basis, local_inv, onehot, coarse_inv, table)
            fresh = residual_product(residual, precond)
            direction = precond + fresh / rz_now * direction
            rz_now = fresh
    return (solution, residual)


def solution(mesh):
    in_specs = (
        P("sub", "col", None, None),
        P("sub", "col", None, None),
        P("sub", "col", None, None),
        P("sub", "col", None, None),
        P("sub", None, None),
        P("sub", "col", None),
        P("sub", "col", None),
    )
    out_specs = (P("sub", "col", None, None), P("sub", "col", None, None))
    return jax.shard_map(body, mesh=mesh, in_specs=in_specs, out_specs=out_specs, check_vma=False)
```

profile of v0, /device:TPU:6, one launch (start us, length us, event | category | flops | bytes accessed | tf_op | source)
XLA Modules:
  0.0 639.9 jit_solution(8085112738998965799)
XLA Ops:
  7.2 3.8 fusion.26
  25.2 10.9 %collective-permute-done = f32[1,2,3,128,256]{4,3,2,1,0:T(8,128)} collective-permute-done((f32[1,2,3,128,256]{4,3,2,1,0:T(8,128)}, f32[1,2,3,128,256]{4,3,2,1,0:T(8,128)}, u32[]{:S(2)}, u32[]{:S(2)}) %collective-permute-start) | collective-permute-done | bytes 786464 | tf_op jit(solution)/shard_map/ppermute | solution.py:17
  44.3 4.7 concatenate.47
  58.7 10.6 %fusion.6 = f32[2,256,1024]{2,1,0:T(8,128)} fusion(f32[1,2,1024,1024]{3,2,1,0:T(8,128)} %param.9, f32[1,2,1024,256]{2,3,1,0:T(8,128)S(1)} %add.55), kind=kOutput, calls=%fused_computation.6 | convolution fusion | flops 6442975232 | bytes 12582912 | tf_op jit(solution)/shard_map/rcij,rcjn->rcin/dot_general | solution.py:53
  69.3 35.3 %all-reduce.4.cloned.1.call-done = f32[192,256]{1,0:T(8,128)} async-done(((f32[192,256]{1,0:T(8,128)}), f32[192,256]{1,0:T(8,128)}) %all-reduce.4.cloned.1.call-update) | async-done | bytes 196624 | tf_op jit(solution)/shard_map/psum | solution.py:50
  106.1 3.5 convolution_add_fusion.1
  111.6 3.1 copy.58
  132.2 16.1 %collective-permute-done.2 = f32[1,2,3,128,256]{4,3,2,1,0:T(8,128)} collective-permute-done((f32[1,2,3,128,256]{4,3,2,1,0:T(8,128)}, f32[1,2,3,128,256]{4,3,2,1,0:T(8,128)}, u32[]{:S(2)}, u32[]{:S(2)}) %collective-permute-start.2) | collective-permute-done | bytes 786464 | tf_op jit(solution)/shard_map/ppermute | solution.py:17
  156.0 6.0 concatenate.50
  165.1 4.0 fusion.64
  174.4 10.4 %fusion.2 = f32[2,256,1024]{2,1,0:T(8,128)S(1)} fusion(f32[1,2,1024,1024]{3,2,1,0:T(8,128)} %param.8, f32[2,1024,256]{1,2,0:T(8,128)S(1)} %get-tuple-element.13), kind=kOutput, calls=%fused_computation.2 | convolution fusion | flops 6442975232 | bytes 12582912 | tf_op jit(solution)/shard_map/rcij,rcjn->rcin/dot_general | solution.py:43
  203.3 4.1 collective-permute-start.5
  207.6 15.6 %collective-permute-done.4 = f32[1,2,3,128,256]{4,3,2,1,0:T(8,128)} collective-permute-done((f32[1,2,3,128,256]{4,3,2,1,0:T(8,128)}, f32[1,2,3,128,256]{4,3,2,1,0:T(8,128)}, u32[]{:S(2)}, u32[]{:S(2)}) %collective-permute-start.4) | collective-permute-done | bytes 786464 | tf_op jit(solution)/shard_map/ppermute | solution.py:17
  230.8 6.0 concatenate.53
  239.9 4.0 fusion.62
  246.5 3.2 multiply_reduce_fusion.1
  249.8 65.9 %all-reduce = (f32[256]{0:T(256)S(1)}, f32[256]{0:T(256)S(1)}) all-reduce(f32[256]{0:T(256)S(1)} %get-tuple-element.40, f32[256]{0:T(256)S(1)} %get-tuple-element.39), channel_id=1, replica_groups=mesh['sub'=32,'col'=4] {'sub','col'}, use_global_device_ids=true, to_apply=%region_2.0 | all-reduce | flops 512 | bytes 4096 | tf_op jit(solution)/shard_map/psum | solution.py:63
  322.7 10.0 %fusion.4 = f32[2,256,1024]{2,1,0:T(8,128)S(1)} fusion(f32[1,2,1024,1024]{3,2,1,0:T(8,128)} %param.9, f32[1,2,1024,256]{2,3,1,0:T(8,128)} %copy-done.4), kind=kOutput, calls=%fused_computation.4 | convolution fusion | flops 6442975232 | bytes 12582912 | tf_op jit(solution)/shard_map/rcij,rcjn->rcin/dot_general | solution.py:53
  332.7 28.7 %all-reduce.6.cloned.1.call-done = f32[192,256]{1,0:T(8,128)} async-done(((f32[192,256]{1,0:T(8,128)}), f32[192,256]{1,0:T(8,128)}) %all-reduce.6.cloned.1.call-update) | async-done | bytes 196624 | tf_op jit(solution)/shard_map/psum | solution.py:50
  377.5 17.0 %collective-permute-done.6 = f32[1,2,3,128,256]{4,3,2,1,0:T(8,128)} collective-permute-done((f32[1,2,3,128,256]{4,3,2,1,0:T(8,128)S(1)}, f32[1,2,3,128,256]{4,3,2,1,0:T(8,128)}, u32[]{:S(2)}, u32[]{:S(2)}) %collective-permute-start.6) | collective-permute-done | bytes 786464 | tf_op jit(solution)/shard_map/ppermute | solution.py:17
  400.0 4.0 concatenate.56
  411.4 3.4 fusion.8
  414.8 64.9 %psum.46 = f32[256]{0:T(256)S(1)} all-reduce(f32[256]{0:T(256)S(1)} %broadcast_multiply_fusion.1), channel_id=1, replica_groups=mesh['sub'=32,'col'=4] {'sub','col'}, use_global_device_ids=true, to_apply=%region_7.0 | all-reduce | flops 256 | bytes 2048 | tf_op jit(solution)/shard_map/psum | solution.py:63
  482.6 10.4 %fusion = f32[2,256,1024]{2,1,0:T(8,128)S(1)} fusion(f32[2,1024,256]{1,2,0:T(8,128)S(1)} %multiply_add_fusion, f32[1,2,1024,1024]{3,2,1,0:T(8,128)} %param.8), kind=kOutput, calls=%fused_computation | convolution fusion | flops 6442450944 | bytes 12582912 | tf_op jit(solution)/shard_map/rcij,rcjn->rcin/dot_general | solution.py:43
  495.1 3.1 copy.86
  510.4 4.3 collective-permute-start.9
  514.9 15.5 %collective-permute-done.8 = f32[1,2,3,128,256]{4,3,2,1,0:T(8,128)} collective-permute-done((f32[1,2,3,128,256]{4,3,2,1,0:T(8,128)}, f32[1,2,3,128,256]{4,3,2,1,0:T(8,128)}, u32[]{:S(2)}, u32[]{:S(2)}) %collective-permute-start.8) | collective-permute-done | bytes 786464 | tf_op jit(solution)/shard_map/ppermute | solution.py:17
  537.4 5.9 concatenate.59
  546.4 3.9 fusion.58
  553.1 3.2 multiply_reduce_fusion
  556.3 65.5 %psum.47 = f32[256]{0:T(256)S(1)} all-reduce(f32[256]{0:T(256)S(1)} %broadcast_multiply_fusion), channel_id=1, replica_groups=mesh['sub'=32,'col'=4] {'sub','col'}, use_global_device_ids=true, to_apply=%region_9.0 | all-reduce | flops 256 | bytes 2048 | tf_op jit(solution)/shard_map/psum | solution.py:67
  621.7 4.7 bitcast_subtract_fusion
  (191 shorter events, 173.3 us)
Async XLA Ops:
  7.2 48.0 %copy-start = (f32[1,2,48,1024]{3,2,1,0:T(8,128)S(1)}, f32[1,2,48,1024]{3,2,1,0:T(8,128)}, u32[]{:S(2)}) copy-start(f32[1,2,48,1024]{3,2,1,0:T(8,128)} %param.10) | copy-start | bytes 1179652
  7.2 97.4 %all-reduce.4.cloned.1.call-start = ((), (), s32[]{:S(2)}) async-start(), calls=%async_computation | async-start | bytes 393216 | tf_op jit(solution)/shard_map/psum | solution.py:50
  14.4 21.7 %collective-permute-start = (f32[1,2,3,128,256]{4,3,2,1,0:T(8,128)}, f32[1,2,3,128,256]{4,3,2,1,0:T(8,128)}, u32[]{:S(2)}, u32[]{:S(2)}) collective-permute-start(f32[1,2,3,128,256]{4,3,2,1,0:T(8,128)} %copy.47), channel_id=1, source_target_pairs={{0,4},{4,8},{8,12},{12,16},{16,20},{20,24},{24,28},{28,32},{32,36}... | collective-permute-start | bytes 2359304 | tf_op jit(solution)/shard_map/ppermute | solution.py:17
  16.0 7.2 %copy-start.12 = (f32[1,2,1024,256]{3,2,1,0:T(8,128)S(1)}, f32[1,2,1024,256]{3,2,1,0:T(8,128)}, u32[]{:S(2)}) copy-start(f32[1,2,1024,256]{3,2,1,0:T(8,128)} %param.7) | copy-start | bytes 6291460
  20.5 19.5 %collective-permute-start.1 = (f32[1,2,3,128,256]{4,3,2,1,0:T(8,128)}, f32[1,2,3,128,256]{4,3,2,1,0:T(8,128)}, u32[]{:S(2)}, u32[]{:S(2)}) collective-permute-start(f32[1,2,3,128,256]{4,3,2,1,0:T(8,128)} %copy.49), channel_id=1, source_target_pairs={{0,124},{4,0},{8,4},{12,8},{16,12},{20,16},{24,20},{28,24},{32,28}... | collective-permute-start | bytes 2359304 | tf_op jit(solution)/shard_map/ppermute | solution.py:17
  44.3 4.7 copy-start.20
  55.2 2.2 copy-start.21
  58.5 46.2 %copy-start.18 = (f32[1,192,192]{2,1,0:T(8,128)S(1)}, f32[1,192,192]{2,1,0:T(8,128)}, u32[]{:S(2)}) copy-start(f32[1,192,192]{2,1,0:T(8,128)} %param.11) | copy-start | bytes 442372
  58.5 303.0 %all-reduce.6.cloned.1.call-start = ((), (), s32[]{:S(2)}) async-start(), calls=%async_computation.1 | async-start | bytes 393216 | tf_op jit(solution)/shard_map/psum | solution.py:50
  109.6 2.0 copy-start.10
  123.6 4.0 copy-start.16
  126.1 5.9 copy-start.13
  126.1 22.2 %collective-permute-start.2 = (f32[1,2,3,128,256]{4,3,2,1,0:T(8,128)}, f32[1,2,3,128,256]{4,3,2,1,0:T(8,128)}, u32[]{:S(2)}, u32[]{:S(2)}) collective-permute-start(f32[1,2,3,128,256]{4,3,2,1,0:T(8,128)} %copy.59), channel_id=1, source_target_pairs={{0,4},{4,8},{8,12},{12,16},{16,20},{20,24},{24,28},{28,32},{32,36}... | collective-permute-start | bytes 2359304 | tf_op jit(solution)/shard_map/ppermute | solution.py:17
  129.1 22.7 %collective-permute-start.3 = (f32[1,2,3,128,256]{4,3,2,1,0:T(8,128)}, f32[1,2,3,128,256]{4,3,2,1,0:T(8,128)}, u32[]{:S(2)}, u32[]{:S(2)}) collective-permute-start(f32[1,2,3,128,256]{4,3,2,1,0:T(8,128)} %copy.61), channel_id=1, source_target_pairs={{0,124},{4,0},{8,4},{12,8},{16,12},{20,16},{24,20},{28,24},{32,28}... | collective-permute-start | bytes 2359304 | tf_op jit(solution)/shard_map/ppermute | solution.py:17
  174.3 10.5 %copy-start.2 = (f32[2,1024,256]{1,2,0:T(8,128)}, f32[2,1024,256]{1,2,0:T(8,128)S(1)}, u32[]{:S(2)}) copy-start(f32[2,1024,256]{1,2,0:T(8,128)S(1)} %get-tuple-element.13) | copy-start | bytes 6291460
  184.8 2.0 copy-start.6
  198.8 3.0 copy-start.17
  201.3 6.1 copy-start.14
  201.3 21.9 %collective-permute-start.4 = (f32[1,2,3,128,256]{4,3,2,1,0:T(8,128)}, f32[1,2,3,128,256]{4,3,2,1,0:T(8,128)}, u32[]{:S(2)}, u32[]{:S(2)}) collective-permute-start(f32[1,2,3,128,256]{4,3,2,1,0:T(8,128)} %copy.68), channel_id=1, source_target_pairs={{0,4},{4,8},{8,12},{12,16},{16,20},{20,24},{24,28},{28,32},{32,36}... | collective-permute-start | bytes 2359304 | tf_op jit(solution)/shard_map/ppermute | solution.py:17
  203.3 23.3 %collective-permute-start.5 = (f32[1,2,3,128,256]{4,3,2,1,0:T(8,128)}, f32[1,2,3,128,256]{4,3,2,1,0:T(8,128)}, u32[]{:S(2)}, u32[]{:S(2)}) collective-permute-start(f32[1,2,3,128,256]{4,3,2,1,0:T(8,128)} %copy.70), channel_id=1, source_target_pairs={{0,124},{4,0},{8,4},{12,8},{16,12},{20,16},{24,20},{28,24},{32,28}... | collective-permute-start | bytes 2359304 | tf_op jit(solution)/shard_map/ppermute | solution.py:17
  322.7 38.8 %copy-start.19 = (f32[1,192,192]{2,1,0:T(8,128)S(1)}, f32[1,192,192]{2,1,0:T(8,128)}, u32[]{:S(2)}) copy-start(f32[1,192,192]{2,1,0:T(8,128)} %param.11) | copy-start | bytes 442372
  364.9 1.9 copy-start.5
  372.4 22.1 %collective-permute-start.6 = (f32[1,2,3,128,256]{4,3,2,1,0:T(8,128)S(1)}, f32[1,2,3,128,256]{4,3,2,1,0:T(8,128)}, u32[]{:S(2)}, u32[]{:S(2)}) collective-permute-start(f32[1,2,3,128,256]{4,3,2,1,0:T(8,128)S(1)} %copy.78), channel_id=1, source_target_pairs={{0,4},{4,8},{8,12},{12,16},{16,20},{20,24},{24,28},{28,32},{32,36}... | collective-permute-start | bytes 2359304 | tf_op jit(solution)/shard_map/ppermute | solution.py:17
  374.6 22.6 %collective-permute-start.7 = (f32[1,2,3,128,256]{4,3,2,1,0:T(8,128)S(1)}, f32[1,2,3,128,256]{4,3,2,1,0:T(8,128)}, u32[]{:S(2)}, u32[]{:S(2)}) collective-permute-start(f32[1,2,3,128,256]{4,3,2,1,0:T(8,128)S(1)} %copy.80), channel_id=1, source_target_pairs={{0,124},{4,0},{8,4},{12,8},{16,12},{20,16},{24,20},{28,24},{32,28}... | collective-permute-start | bytes 2359304 | tf_op jit(solution)/shard_map/ppermute | solution.py:17
  411.4 68.3 %copy-start.3 = (f32[2,1024,256]{1,2,0:T(8,128)S(1)}, f32[2,1024,256]{1,2,0:T(8,128)}, u32[]{:S(2)}) copy-start(f32[2,1024,256]{1,2,0:T(8,128)} %copy-done.2) | copy-start | bytes 6291460
  482.6 10.5 %copy-start.7 = (f32[2,1024,256]{1,2,0:T(8,128)}, f32[2,1024,256]{1,2,0:T(8,128)S(1)}, u32[]{:S(2)}) copy-start(f32[2,1024,256]{1,2,0:T(8,128)S(1)} %multiply_add_fusion) | copy-start | bytes 6291460
  508.8 5.8 copy-start.15
  508.8 21.6 %collective-permute-start.8 = (f32[1,2,3,128,256]{4,3,2,1,0:T(8,128)}, f32[1,2,3,128,256]{4,3,2,1,0:T(8,128)}, u32[]{:S(2)}, u32[]{:S(2)}) collective-permute-start(f32[1,2,3,128,256]{4,3,2,1,0:T(8,128)} %copy.87), channel_id=1, source_target_pairs={{0,4},{4,8},{8,12},{12,16},{16,20},{20,24},{24,28},{28,32},{32,36}... | collective-permute-start | bytes 2359304 | tf_op jit(solution)/shard_map/ppermute | solution.py:17
  510.4 22.8 %collective-permute-start.9 = (f32[1,2,3,128,256]{4,3,2,1,0:T(8,128)}, f32[1,2,3,128,256]{4,3,2,1,0:T(8,128)}, u32[]{:S(2)}, u32[]{:S(2)}) collective-permute-start(f32[1,2,3,128,256]{4,3,2,1,0:T(8,128)} %copy.89), channel_id=1, source_target_pairs={{0,124},{4,0},{8,4},{12,8},{16,12},{20,16},{24,20},{28,24},{32,28}... | collective-permute-start | bytes 2359304 | tf_op jit(solution)/shard_map/ppermute | solution.py:17
  621.7 4.7 copy-start.8
  628.0 3.0 copy-start.11
  628.0 4.8 copy-start.1
  (2 other events, 3.3 us)
Sparse Core Ops, SparseCore 0:
  58.6 45.9 all-reduce.3
  322.8 38.5 all-reduce.5
where the time goes:
time: 650 us; the launch traced here: 640 us
  blocking collectives  196 us (30%)
  local copies, waits for them, and re-layouts  147 us (23%)
  waiting for transfers between devices  140 us (22%)
  matrix products  84.5 us (13%)
  other arithmetic  35.5 us (5%)
  starting transfers between devices  22.1 us (3%)
  between operations  14.9 us (2%)
    psum x2, blocking collectives, residual_product(): return lax.psum(partial_inner(residual, precond), ('sub', 'col'))  131 us
    ppermute x10, waiting for transfers between devices, from_behind(): return lax.ppermute(value, axis, pairs)  75.6 us
    psum x1, blocking collectives, curvature_product(): return lax.psum(partial_inner(direction, image), ('sub', 'col'))  65.5 us
    psum x2, waiting for transfers between devices, precondition(): assembled = lax.psum(own, 'col')  64 us
    concatenate x5, local copies, waits for them, and re-layouts, neighbour_sum(): jnp.concatenate([from_prior[:, :, 0:2], from_next[:, :, 0:2], by_role[:,...  26.6 us
    another operation x8, local copies, waits for them, and re-layouts  23.4 us
    unnamed x61, local copies, waits for them, and re-layouts  23.2 us
    ppermute x10, starting transfers between devices, from_behind(): return lax.ppermute(value, axis, pairs)  21.8 us
  transfers between devices with their start and end apart: 12, of which 8 were waited for; matrix products, arithmetic and copies ran while one was open for 8% of the time, Pallas kernels for 0%

commit v1 on v0

v1 whole, which is shorter than its diff:
```python
import jax
import jax.numpy as jnp
from jax import lax
from jax.experimental import pallas as pl
from jax.experimental.pallas import tpu as pltpu
from jax.sharding import PartitionSpec as P

MESH = pl.DeviceIdType.MESH
F32 = jnp.float32
BF16 = jnp.bfloat16

NB = 8
BLOCK = 128
NI = 1024
NPRIM = 48
NCG = 192
HALF = 128
NG = 256

KINDS = ((0, 256, 0), (256, 512, 1), (512, 640, 0), (640, 768, 1))


def role_at(i):
    return i + 2 * (i // 4) * (1 - 2 * ((i % 4) // 2))


def split(value):
    hi = value.astype(BF16)
    lo = (value - hi.astype(F32)).astype(BF16)
    return hi, lo


def fold(value):
    return value.reshape(value.shape[0] // 8, 8, HALF).sum(axis=0)


def kernel(
    roles, primal, loads, schur, linv, basis, cinv, sol_out, res_out,
    raw0, raw1, ld, r, y, s, d, x, rb, stag0, stag1, mh, ml, vs, bas, bpad, bh, bl, cin, cinp, gh, gl,
    pbuf, selt, rowsall, arz, arx,
    ld_sem, st_sem, bas_sem, cin_sem, out_sem, ss, rs, ps, pr, cs, cr, azs, azr, axs, axr,
):
    raw, stag = (raw0, raw1), (stag0, stag1)
    me = lax.axis_index("sub")
    col = lax.axis_index("col")
    up, dn = lax.rem(me + 1, 32), lax.rem(me + 31, 32)
    p16, zlo = lax.rem(me, 16), me // 16
    g8 = zlo * 4 + col
    mate = col + 1 - 2 * lax.rem(col, 2)
    opp = lax.rem(col + 2, 4)
    diag = lax.rem(mate + 2, 4)

    load_in = [
        pltpu.make_async_copy(loads.at[0, :, :, :, pl.ds(h * HALF, HALF)], raw[h], ld_sem.at[h]) for h in range(2)
    ]
    def columns(src, c, first):
        return [
            pltpu.make_async_copy(src.at[0, c, :, :, pl.ds(j * BLOCK, BLOCK)], stag[c].at[j], st_sem.at[first + c, j])
            for j in range(NB)
        ]

    linv_in = [columns(linv, c, 0) for c in range(2)]
    schur_in = [columns(schur, c, 2) for c in range(2)]
    basis_in = [
        pltpu.make_async_copy(basis.at[0, :, :, pl.ds(j * BLOCK, BLOCK)], bas.at[j], bas_sem.at[j]) for j in range(NB)
    ]
    cinv_in = pltpu.make_async_copy(cinv.at[0], cin, cin_sem)
    load_in[0].start()
    load_in[1].start()
    for copy in basis_in + linv_in[0] + [cinv_in] + linv_in[1]:
        copy.start()

    def z_dev(t):
        return ((t // 4) * 16 + p16, lax.rem(t, 4))

    def xy_dev(t):
        return (zlo * 16 + t, col)

    rowsall[...] = jnp.zeros(rowsall.shape, F32)
    barrier = pltpu.get_barrier_semaphore()

    def greet_z(k, _):
        pl.semaphore_signal(barrier, inc=1, device_id=z_dev(lax.rem(g8 + k, 8)), device_id_type=MESH)
        return 0

    def greet_xy(k, _):
        pl.semaphore_signal(barrier, inc=1, device_id=xy_dev(lax.rem(p16 + k, 16)), device_id_type=MESH)
        return 0

    pl.semaphore_signal(barrier, inc=1, device_id=(up, col), device_id_type=MESH)
    pl.semaphore_signal(barrier, inc=1, device_id=(dn, col), device_id_type=MESH)
    lax.fori_loop(1, 8, greet_z, 0)
    lax.fori_loop(1, 16, greet_xy, 0)

    def block_rows(index):
        return pl.ds(pl.multiple_of(index * BLOCK, BLOCK), BLOCK)

    def gather_loads(h):
        for c in range(2):
            for i in range(NB):
                ld[h, c, i * BLOCK : (i + 1) * BLOCK, :] = raw[h][c, roles[0, c, role_at(i)]]

    def face(buf, n, h, c, kind):
        first, last, way = KINDS[kind]
        to = c if kind < 2 else 1 - c
        rows = pl.ds(0, 256) if kind < 2 else pl.ds(256, 128)
        return pltpu.make_async_remote_copy(
            src_ref=buf.at[h, c, pl.ds(first, last - first), :],
            dst_ref=rb.at[n, way, h, to, rows, :],
            send_sem=ss.at[n, h, c * 4 + kind],
            recv_sem=rs.at[n, h, to * 4 + kind],
            device_id=(up if way else dn, col),
            device_id_type=MESH,
        )

    HEAD = ((0, 0), (0, 1))
    TAIL = ((1, 0), (1, 1), (0, 2), (0, 3), (1, 2), (1, 3))

    def send(buf, n, h, which):
        for c, kind in which:
            face(buf, n, h, c, kind).start()

    def receive(buf, n, h):
        for c, kind in HEAD + TAIL:
            face(buf, n, h, c, kind).wait_recv()

    def sent(buf, n, h):
        for c, kind in HEAD + TAIL:
            face(buf, n, h, c, kind).wait_send()

    def summed(buf, n, h, c):
        yield slice(0, 256), buf[h, c, 0:256, :] + rb[n, 1, h, c, 0:256, :]
        yield slice(256, 512), buf[h, c, 256:512, :] + rb[n, 0, h, c, 0:256, :]
        yield slice(512, 640), buf[h, c, 512:640, :] + rb[n, 1, h, c, 256:384, :]
        yield slice(640, 768), buf[h, c, 640:768, :] + rb[n, 0, h, c, 256:384, :]
        yield slice(768, 1024), buf[h, c, 768:1024, :] + buf[h, 1 - c, 768:1024, :]

    def z_copy(q, t_src, t_dst, k):
        return pltpu.make_async_remote_copy(
            src_ref=arz.at[q, t_src], dst_ref=arz.at[q, t_src], send_sem=azs.at[q, k], recv_sem=azr.at[q, t_src],
            device_id=z_dev(t_dst), device_id_type=MESH,
        )

    def xy_copy(q, t_src, t_dst, k):
        return pltpu.make_async_remote_copy(
            src_ref=arx.at[q, t_src], dst_ref=arx.at[q, t_src], send_sem=axs.at[q, k], recv_sem=axr.at[q, t_src],
            device_id=xy_dev(t_dst), device_id_type=MESH,
        )

    def reduce_begin(q, first, second):
        arz[q, g8, 0:1, :] = jnp.sum(first, axis=0, keepdims=True)
        arz[q, g8, 1:2, :] = jnp.sum(second, axis=0, keepdims=True)

        def go(k, _):
            z_copy(q, g8, lax.rem(g8 + k, 8), k).start()
            return 0

        lax.fori_loop(1, 8, go, 0)

    def reduce_middle(q):
        def hold(k, _):
            t = lax.rem(g8 + k, 8)
            z_copy(q, t, t, k).wait_recv()
            return 0

        lax.fori_loop(1, 8, hold, 0)
        arx[q, p16] = jnp.sum(arz[q], axis=0)

        def go(k, _):
            xy_copy(q, p16, lax.rem(p16 + k, 16), k).start()
            return 0

        lax.fori_loop(1, 16, go, 0)

    def reduce_end(q):
        def hold(k, _):
            t = lax.rem(p16 + k, 16)
            xy_copy(q, t, t, k).wait_recv()
            xy_copy(q, p16, t, k).wait_send()
            return 0

        lax.fori_loop(1, 16, hold, 0)

        def drop(k, _):
            z_copy(q, g8, lax.rem(g8 + k, 8), k).wait_send()
            return 0

        lax.fori_loop(1, 8, drop, 0)
        total = jnp.sum(arx[q], axis=0)
        return total[0:1, :], total[1:2, :]

    def rows_copy(m, h, slot, to, k):
        return pltpu.make_async_remote_copy(
            src_ref=rowsall.at[m, h, slot, :, pl.ds(0, NPRIM), :],
            dst_ref=rowsall.at[m, h, slot, :, pl.ds(0, NPRIM), :],
            send_sem=cs.at[m, h, k], recv_sem=cr.at[m, h, k],
            device_id=(me, to), device_id_type=MESH,
        )

    def primal_copy(slot, to, k):
        return pltpu.make_async_remote_copy(
            src_ref=pbuf.at[slot], dst_ref=pbuf.at[slot], send_sem=ps.at[k], recv_sem=pr.at[k],
            device_id=(me, to), device_id_type=MESH,
        )

    def convert(m, c, scale):
        def rows(i, _):
            src = roles[0, c, role_at(i)]
            for j in range(NB):
                hi, lo = split(stag[c][roles[0, c, role_at(j)], src] * scale)
                mh[m, block_rows(i), j * BLOCK : (j + 1) * BLOCK] = hi
                ml[m, block_rows(i), j * BLOCK : (j + 1) * BLOCK] = lo
            return 0

        lax.fori_loop(0, NB, rows, 0)

    pbuf[col] = jnp.full((8, HALF), -1, jnp.int32)
    pbuf[col, 0:2, 0:NPRIM] = primal[0]
    load_in[0].wait()
    gather_loads(0)
    pl.semaphore_wait(barrier, 24)
    primal_copy(col, mate, 0).start()
    primal_copy(col, opp, 1).start()
    primal_copy(col, diag, 2).start()
    send(ld, 0, 0, HEAD + TAIL)
    load_in[1].wait()
    gather_loads(1)
    send(ld, 0, 1, HEAD)

    bpad[...] = jnp.zeros(bpad.shape, F32)
    cinp[...] = jnp.zeros(cinp.shape, F32)
    for copy in basis_in:
        copy.wait()
    cinv_in.wait()
    cinp[0:NCG, 0:NCG] = cin[...]
    for c in range(2):
        for j in range(NB):
            piece = bas[roles[0, c, role_at(j)], c] * 0.5
            bpad[c, 0:NPRIM, j * BLOCK : (j + 1) * BLOCK] = piece
            hi, lo = split(piece)
            bh[c, :, j * BLOCK : (j + 1) * BLOCK] = hi
            bl[c, :, j * BLOCK : (j + 1) * BLOCK] = lo
    for c in range(2):
        for copy in linv_in[c]:
            copy.wait()
        convert(c, c, 0.25)
        for copy in schur_in[c]:
            copy.start()
    index = lax.broadcasted_iota(jnp.int32, (NG, HALF), 0)
    for c in range(2):
        own = (index == pbuf[col, c : c + 1, :]).astype(F32)

        def assemble(j, _):
            at = block_rows(j)
            part = jnp.dot(own, bpad[c, :, at], precision=lax.Precision.HIGHEST, preferred_element_type=F32)
            hi, lo = split(part.T)
            gh[c, at, :] = hi
            gl[c, at, :] = lo
            return 0

        lax.fori_loop(0, NB, assemble, 0)
    for k, slot in enumerate((mate, opp, diag)):
        primal_copy(slot, col, k).wait_recv()
        primal_copy(col, slot, k).wait_send()
    for slot in range(4):
        for c in range(2):
            at = slot * 2 + c
            selt[:, at * HALF : (at + 1) * HALF] = (index == pbuf[slot, c : c + 1, :]).astype(F32).astype(BF16)
    for copy in schur_in[0]:
        copy.wait()
    convert(2, 0, 1.0)

    def apply(base, h, dst, other):
        def tile(index, acc):
            c, t = index // 4, lax.rem(index, 4)
            rows = pl.ds(pl.multiple_of(t * 256, 256), 256)
            wide = jnp.dot(mh[base + c, rows, :], vs[c], preferred_element_type=F32)
            low = jnp.dot(ml[base + c, rows, :], vs[c, :, 0:HALF], preferred_element_type=F32)
            out = wide[:, 0:HALF] + wide[:, HALF:] + low
            dst[h, c, rows, :] = out
            if other is None:
                return acc
            return acc + fold(out * other[h, c, rows, :])

        return lax.fori_loop(0, 8, tile, jnp.zeros((8, HALF), F32))

    def operand(c, rows, value):
        hi, lo = split(value)
        vs[c, rows, 0:HALF] = hi
        vs[c, rows, HALF:] = lo

    def precondition(m, h, flush):
        for c in range(2):
            wide = jnp.dot(bh[c], vs[c], preferred_element_type=F32)
            low = jnp.dot(bl[c], vs[c, :, 0:HALF], preferred_element_type=F32)
            rowsall[m, h, col, c, 0:NPRIM, :] = wide[:, 0:HALF] + wide[:, HALF:] + low
        rows_copy(m, h, col, opp, 1).start()
        rows_copy(m, h, col, mate, 0).start()
        flush()
        apply(0, h, y, None)
        rows_copy(m, h, opp, col, 1).wait_recv()
        rows_copy(m, h, opp, mate, 2).start()
        rows_copy(m, h, mate, col, 0).wait_recv()
        rows_copy(m, h, diag, col, 2).wait_recv()
        hi, lo = split(rowsall[m, h].reshape(8 * HALF, HALF))
        coarse = jnp.dot(selt[...], jnp.concatenate([hi, lo], axis=1), preferred_element_type=F32)
        coarse = coarse[:, 0:HALF] + coarse[:, HALF:]
        spread = jnp.dot(cinp[...], coarse, precision=lax.Precision.HIGHEST, preferred_element_type=F32)
        hi, lo = split(spread)
        both = jnp.concatenate([hi, lo], axis=1)

        def tile(index, acc):
            c, t = index // 4, lax.rem(index, 4)
            rows = pl.ds(pl.multiple_of(t * 256, 256), 256)
            wide = jnp.dot(gh[c, rows, :], both, preferred_element_type=F32)
            low = jnp.dot(gl[c, rows, :], hi, preferred_element_type=F32)
            out = y[h, c, rows, :] + (wide[:, 0:HALF] + wide[:, HALF:] + low)
            y[h, c, rows, :] = out
            return acc + fold(out * r[h, c, rows, :])

        acc = lax.fori_loop(0, 8, tile, jnp.zeros((8, HALF), F32))
        for k, (slot, to) in enumerate(((col, mate), (col, opp), (opp, mate))):
            rows_copy(m, h, slot, to, k).wait_send()
        return acc

    zero = jnp.zeros((8, HALF), F32)
    nothing = lambda: None

    rz_part = [None, None]
    for h in range(2):
        receive(ld, 0, h)
        for c in range(2):
            for rows, value in summed(ld, 0, h, c):
                r[h, c, rows, :] = value
                operand(c, rows, value)
        rz_part[h] = precondition(0, h, (lambda: send(ld, 0, 1, TAIL)) if h == 0 else (lambda: send(y, 1, 0, TAIL)))
        send(y, 1, h, HEAD)
        if h == 0:
            for copy in schur_in[1]:
                copy.wait()
            convert(3, 1, 1.0)
    send(y, 1, 1, TAIL)

    for h in range(2):
        receive(y, 1, h)
        for c in range(2):
            for rows, value in summed(y, 1, h, c):
                d[h, c, rows, :] = value
                operand(c, rows, value)
        part = apply(2, h, s, d)
        send(s, 2, h, HEAD)
        reduce_begin(h, rz_part[h], part)
        reduce_middle(h)
        if h == 0:
            send(s, 2, 0, TAIL)

    rz_now = [None, None]
    for h in range(2):
        receive(s, 2, h)
        rz_now[h], curve = reduce_end(h)
        alpha = rz_now[h] / curve
        for c in range(2):
            for rows, value in summed(s, 2, h, c):
                value = r[h, c, rows, :] - alpha * value
                r[h, c, rows, :] = value
                operand(c, rows, value)
                x[h, c, rows, :] = alpha * d[h, c, rows, :]
        sent(y, 1, h)
        part = precondition(1, h, (lambda: send(s, 2, 1, TAIL)) if h == 0 else (lambda: send(y, 3, 0, TAIL)))
        send(y, 3, h, HEAD)
        reduce_begin(2 + h, part, zero)
        reduce_middle(2 + h)
    send(y, 3, 1, TAIL)

    rz_new = [None, None]
    for h in range(2):
        receive(y, 3, h)
        rz_new[h], _ = reduce_end(2 + h)
        beta = rz_new[h] / rz_now[h]
        for c in range(2):
            for rows, value in summed(y, 3, h, c):
                value = value + beta * d[h, c, rows, :]
                d[h, c, rows, :] = value
                operand(c, rows, value)
        sent(s, 2, h)
        part = apply(2, h, s, d)
        send(s, 4, h, HEAD)
        reduce_begin(4 + h, part, zero)
        reduce_middle(4 + h)
        send(s, 4, h, TAIL)

    sol_copy = [pltpu.make_async_copy(x.at[h], sol_out.at[h], out_sem.at[h]) for h in range(2)]
    res_copy = [pltpu.make_async_copy(r.at[h], res_out.at[h], out_sem.at[2 + h]) for h in range(2)]
    for h in range(2):
        sent(ld, 0, h)
        curve, _ = reduce_end(4 + h)
        alpha = rz_new[h] / curve
        for c in range(2):
            x[h, c] = x[h, c] + alpha * d[h, c]
        sol_copy[h].start()
        receive(s, 4, h)
        for c in range(2):
            for rows, value in summed(s, 4, h, c):
                r[h, c, rows, :] = r[h, c, rows, :] - alpha * value
        res_copy[h].start()
    for h in range(2):
        sent(y, 3, h)
        sent(s, 4, h)
        sol_copy[h].wait()
        res_copy[h].wait()


def place(roles, sol_in, res_in, sol_out, res_out):
    for h in range(2):
        sol_out[0, 0, :, h * HALF : (h + 1) * HALF] = sol_in[h, 0]
        res_out[0, 0, :, h * HALF : (h + 1) * HALF] = res_in[h, 0]


def body(loads, schur, local_inv, basis, coarse_inv, primal, block_roles):
    vec = pltpu.VMEM((2, 2, NI, HALF), F32)
    dma = pltpu.SemaphoreType.DMA
    any_space = pl.BlockSpec(memory_space=pl.ANY)
    half = jax.ShapeDtypeStruct((2, 2, NI, HALF), F32)
    sol, res = pl.pallas_call(
        kernel,
        out_shape=(half, half),
        in_specs=[pl.BlockSpec(memory_space=pltpu.SMEM), pl.BlockSpec(memory_space=pltpu.VMEM)] + [any_space] * 5,
        out_specs=(any_space, any_space),
        scratch_shapes=[
            pltpu.VMEM((2, NB, BLOCK, HALF), F32), pltpu.VMEM((2, NB, BLOCK, HALF), F32),
            vec, vec, vec, vec, vec, vec,
            pltpu.VMEM((5, 2, 2, 2, 384, HALF), F32),
            pltpu.VMEM((NB, NB, BLOCK, BLOCK), F32), pltpu.VMEM((NB, NB, BLOCK, BLOCK), F32),
            pltpu.VMEM((4, NI, NI), BF16),
            pltpu.VMEM((4, NI, NI), BF16),
            pltpu.VMEM((2, NI, 2 * HALF), BF16),
            pltpu.VMEM((NB, 2, NPRIM, BLOCK), F32),
            pltpu.VMEM((2, HALF, NI), F32),
            pltpu.VMEM((2, NPRIM, NI), BF16),
            pltpu.VMEM((2, NPRIM, NI), BF16),
            pltpu.VMEM((NCG, NCG), F32),
            pltpu.VMEM((NG, NG), F32),
            pltpu.VMEM((2, NI, NG), BF16),
            pltpu.VMEM((2, NI, NG), BF16),
            pltpu.VMEM((4, 8, HALF), jnp.int32),
            pltpu.VMEM((NG, 8 * HALF), BF16),
            pltpu.VMEM((2, 2, 4, 2, HALF, HALF), F32),
            pltpu.VMEM((6, 8, 2, HALF), F32),
            pltpu.VMEM((6, 16, 2, HALF), F32),
            dma((2,)), dma((4, NB)), dma((NB,)), dma, dma((4,)),
            dma((5, 2, 8)), dma((5, 2, 8)),
            dma((3,)), dma((3,)),
            dma((2, 2, 3)), dma((2, 2, 3)),
            dma((6, 8)), dma((6, 8)), dma((6, 16)), dma((6, 16)),
        ],
        compiler_params=pltpu.CompilerParams(
            collective_id=0, has_side_effects=True, vmem_limit_bytes=62 * 2**20
        ),
    )(
        block_roles,
        primal,
        loads.reshape(1, 2, NB, BLOCK, 2 * HALF),
        schur.reshape(1, 2, NB, BLOCK, NI),
        local_inv.reshape(1, 2, NB, BLOCK, NI),
        basis,
        coarse_inv,
    )
    out = jax.ShapeDtypeStruct(loads.shape, F32)
    held = pl.BlockSpec((2, 1, BLOCK, HALF), lambda c, i, roles: (0, c, i, 0))
    given = pl.BlockSpec((1, 1, BLOCK, 2 * HALF), lambda c, i, roles: (0, c, roles[0, c, role_at(i)], 0))
    return pl.pallas_call(
        place,
        out_shape=(out, out),
        grid_spec=pltpu.PrefetchScalarGridSpec(
            num_scalar_prefetch=1, grid=(2, NB), in_specs=[held, held], out_specs=(given, given)
        ),
    )(block_roles, sol, res)


def solution(mesh):
    in_specs = (
        P("sub", "col", None, None),
        P("sub", "col", None, None),
        P("sub", "col", None, None),
        P("sub", "col", None, None),
        P("sub", None, None),
        P("sub", "col", None),
        P("sub", "col", None),
    )
    out_specs = (P("sub", "col", None, None), P("sub", "col", None, None))
    return jax.shard_map(body, mesh=mesh, in_specs=in_specs, out_specs=out_specs, check_vma=False)
```

time: 650 us -> 171 us (0.26)
  the two profiles are of different devices: /device:TPU:6 before, /device:TPU:1 now
where the time goes in v1:
time: 171 us
  Pallas kernels  170 us (99%)
    pallas_call x1, Pallas kernels, body(): pl.pallas_call(kernel, out_shape=(half, half), in_specs=[pl.BlockSpec(mem...  159 us
    pallas_call x1, Pallas kernels, body(): pl.pallas_call(place, out_shape=(out, out), grid_spec=pltpu.PrefetchScala...  11 us

profile of v1, /device:TPU:1, one launch (start us, length us, event | category | flops | bytes accessed | tf_op | source)
XLA Modules:
  0.0 170.6 jit_solution(11605638881805934494)
XLA Ops:
  0.6 158.9 %shard_map.86 = (f32[2,2,1024,128]{3,2,1,0:T(8,128)}, f32[2,2,1024,128]{3,2,1,0:T(8,128)}) custom-call(s32[1,2,8]{2,1,0:T(2,128)} %roles.3, s32[1,2,48]{2,1,0:T(2,128)} %primal.1, f32[1,2,8,128,256]{4,3,2,1,0:T(8,128)} %bitcast.5, f32[1,2,8,128,1024]{4,3,2,1,0:T(8,128)} %bitcast.3, f32[1,2,8,128,1024]{4,3,2,1,0:T(8,128)} %bitcast.4, ...), custom_call_target="tpu_custom_call" | custom-call | tf_op jit(solution)/shard_map/pallas_call | solution.py:424
  159.5 11.0 %shard_map.87 = (f32[1,2,1024,256]{3,2,1,0:T(8,128)}, f32[1,2,1024,256]{3,2,1,0:T(8,128)}) custom-call(s32[1,2,8]{2,1,0:T(2,128)} %roles.3, f32[2,2,1024,128]{3,2,1,0:T(8,128)} %get-tuple-element.4.sol_in, f32[2,2,1024,128]{3,2,1,0:T(8,128)} %get-tuple-element.5.res_in), custom_call_target="tpu_custom_call" | custom-call | tf_op jit(solution)/shard_map/pallas_call | solution.py:471

commit v2 on v1

--- a/solution.py
+++ b/solution.py
@@ -37,10 +37,11 @@
 def kernel(
     roles, primal, loads, schur, linv, basis, cinv, sol_out, res_out,
     raw0, raw1, ld, r, y, s, d, x, rb, stag0, stag1, mh, ml, vs, bas, bpad, bh, bl, cin, cinp, gh, gl,
-    pbuf, selt, rowsall, arz, arx,
-    ld_sem, st_sem, bas_sem, cin_sem, out_sem, ss, rs, ps, pr, cs, cr, azs, azr, axs, axr,
+    pbuf, selt, rowsall, arz, arx, arw,
+    ld_sem, st_sem, bas_sem, cin_sem, out_sem, ss, rs, ps, pr, cs, cr, azs, azr, axs, axr, aws, awr,
 ):
     raw, stag = (raw0, raw1), (stag0, stag1)
+    r2, x2 = r.reshape(2, 2, NI, HALF), x.reshape(2, 2, NI, HALF)
     me = lax.axis_index("sub")
     col = lax.axis_index("col")
     up, dn = lax.rem(me + 1, 32), lax.rem(me + 31, 32)
@@ -49,6 +50,11 @@
     mate = col + 1 - 2 * lax.rem(col, 2)
     opp = lax.rem(col + 2, 4)
     diag = lax.rem(mate + 2, 4)
+    inner = (p16 > 0) & (p16 < 15)
+    edge = (p16 == 0) | (p16 == 15)
+    relay = (p16 == 4) | (p16 == 11)
+    partner = zlo * 16 + jnp.where(p16 == 0, 4, jnp.where(p16 == 4, 0, jnp.where(p16 == 15, 11, 15)))
+    crossing = (p16 == 0, p16 == 15)
 
     load_in = [
         pltpu.make_async_copy(loads.at[0, :, :, :, pl.ds(h * HALF, HALF)], raw[h], ld_sem.at[h]) for h in range(2)
@@ -114,11 +120,23 @@
         )
 
     HEAD = ((0, 0), (0, 1))
-    TAIL = ((1, 0), (1, 1), (0, 2), (0, 3), (1, 2), (1, 3))
+    SOON = ((0, 2), (0, 3))
+    TAIL = SOON + ((1, 0), (1, 1), (1, 2), (1, 3))
 
     def send(buf, n, h, which):
         for c, kind in which:
             face(buf, n, h, c, kind).start()
+
+    def send_rest(buf, n, h, over_z):
+        for c, kind in TAIL:
+            z_way = crossing[KINDS[kind][2]]
+            if (c, kind) in SOON:
+                if not over_z:
+                    face(buf, n, h, c, kind).start()
+            else:
+                @pl.when(z_way if over_z else jnp.logical_not(z_way))
+                def _():
+                    face(buf, n, h, c, kind).start()
 
     def receive(buf, n, h):
         for c, kind in HEAD + TAIL:
@@ -151,43 +169,78 @@
         arz[q, g8, 0:1, :] = jnp.sum(first, axis=0, keepdims=True)
         arz[q, g8, 1:2, :] = jnp.sum(second, axis=0, keepdims=True)
 
-        def go(k, _):
-            z_copy(q, g8, lax.rem(g8 + k, 8), k).start()
-            return 0
-
-        lax.fori_loop(1, 8, go, 0)
+        @pl.when(edge)
+        def _():
+            edge_copy(q).start()
+
+        @pl.when(relay)
+        def _():
+            edge_copy(q).wait_recv()
+            arz[q, g8] = arz[q, g8] + arw[q]
+
+        @pl.when(inner)
+        def _():
+            def go(k, _):
+                z_copy(q, g8, lax.rem(g8 + k, 8), k).start()
+                return 0
+
+            lax.fori_loop(1, 8, go, 0)
 
     def reduce_middle(q):
-        def hold(k, _):
-            t = lax.rem(g8 + k, 8)
-            z_copy(q, t, t, k).wait_recv()
-            return 0
-
-        lax.fori_loop(1, 8, hold, 0)
-        arx[q, p16] = jnp.sum(arz[q], axis=0)
-
-        def go(k, _):
-            xy_copy(q, p16, lax.rem(p16 + k, 16), k).start()
-            return 0
-
-        lax.fori_loop(1, 16, go, 0)
+        @pl.when(inner)
+        def _():
+            def hold(k, _):
+                t = lax.rem(g8 + k, 8)
+                z_copy(q, t, t, k).wait_recv()
+                return 0
+
+            lax.fori_loop(1, 8, hold, 0)
+            arx[q, p16] = jnp.sum(arz[q], axis=0)
+
+            def go(k, _):
+                xy_copy(q, p16, lax.rem(p16 + k, 16), k).start()
+                return 0
+
+            lax.fori_loop(1, 16, go, 0)
 
     def reduce_end(q):
         def hold(k, _):
             t = lax.rem(p16 + k, 16)
-            xy_copy(q, t, t, k).wait_recv()
-            xy_copy(q, p16, t, k).wait_send()
+
+            @pl.when((t > 0) & (t < 15))
+            def _():
+                xy_copy(q, t, t, k).wait_recv()
+
             return 0
 
         lax.fori_loop(1, 16, hold, 0)
 
-        def drop(k, _):
-            z_copy(q, g8, lax.rem(g8 + k, 8), k).wait_send()
-            return 0
-
-        lax.fori_loop(1, 8, drop, 0)
-        total = jnp.sum(arx[q], axis=0)
+        @pl.when(edge)
+        def _():
+            edge_copy(q).wait_send()
+
+        @pl.when(inner)
+        def _():
+            def drop_xy(k, _):
+                xy_copy(q, p16, lax.rem(p16 + k, 16), k).wait_send()
+                return 0
+
+            lax.fori_loop(1, 16, drop_xy, 0)
+
+            def drop_z(k, _):
+                z_copy(q, g8, lax.rem(g8 + k, 8), k).wait_send()
+                return 0
+
+            lax.fori_loop(1, 8, drop_z, 0)
+
+        total = jnp.sum(arx[q, 1:15], axis=0)
         return total[0:1, :], total[1:2, :]
+
+    def edge_copy(q):
+        return pltpu.make_async_remote_copy(
+            src_ref=arz.at[q, g8], dst_ref=arw.at[q], send_sem=aws.at[q], recv_sem=awr.at[q],
+            device_id=(partner, col), device_id_type=MESH,
+        )
 
     def rows_copy(m, h, slot, to, k):
         return pltpu.make_async_remote_copy(
@@ -289,17 +342,18 @@
         vs[c, rows, 0:HALF] = hi
         vs[c, rows, HALF:] = lo
 
-    def precondition(m, h, flush):
+    def precondition(m, h, out, waiting):
         for c in range(2):
             wide = jnp.dot(bh[c], vs[c], preferred_element_type=F32)
             low = jnp.dot(bl[c], vs[c, :, 0:HALF], preferred_element_type=F32)
             rowsall[m, h, col, c, 0:NPRIM, :] = wide[:, 0:HALF] + wide[:, HALF:] + low
         rows_copy(m, h, col, opp, 1).start()
         rows_copy(m, h, col, mate, 0).start()
-        flush()
+        send_rest(*waiting, False)
         apply(0, h, y, None)
         rows_copy(m, h, opp, col, 1).wait_recv()
         rows_copy(m, h, opp, mate, 2).start()
+        send_rest(*waiting, True)
         rows_copy(m, h, mate, col, 0).wait_recv()
         rows_copy(m, h, diag, col, 2).wait_recv()
         hi, lo = split(rowsall[m, h].reshape(8 * HALF, HALF))
@@ -314,27 +368,31 @@
             rows = pl.ds(pl.multiple_of(t * 256, 256), 256)
             wide = jnp.dot(gh[c, rows, :], both, preferred_element_type=F32)
             low = jnp.dot(gl[c, rows, :], hi, preferred_element_type=F32)
-            out = y[h, c, rows, :] + (wide[:, 0:HALF] + wide[:, HALF:] + low)
-            y[h, c, rows, :] = out
-            return acc + fold(out * r[h, c, rows, :])
+            value = y[h, c, rows, :] + (wide[:, 0:HALF] + wide[:, HALF:] + low)
+            y[h, c, rows, :] = value
+
+            @pl.when(index == 1)
+            def _():
+                send(y, out, h, HEAD)
+
+            return acc + fold(value * r2[h, c, rows, :])
 
         acc = lax.fori_loop(0, 8, tile, jnp.zeros((8, HALF), F32))
-        for k, (slot, to) in enumerate(((col, mate), (col, opp), (opp, mate))):
-            rows_copy(m, h, slot, to, k).wait_send()
+        rows_copy(m, h, col, mate, 0).wait_send()
+        rows_copy(m, h, opp, mate, 2).wait_send()
+        rows_copy(m, h, col, opp, 1).wait_send()
         return acc
 
     zero = jnp.zeros((8, HALF), F32)
-    nothing = lambda: None
 
     rz_part = [None, None]
     for h in range(2):
         receive(ld, 0, h)
         for c in range(2):
             for rows, value in summed(ld, 0, h, c):
-                r[h, c, rows, :] = value
+                r2[h, c, rows, :] = value
                 operand(c, rows, value)
-        rz_part[h] = precondition(0, h, (lambda: send(ld, 0, 1, TAIL)) if h == 0 else (lambda: send(y, 1, 0, TAIL)))
-        send(y, 1, h, HEAD)
+        rz_part[h] = precondition(0, h, 1, (ld, 0, 1) if h == 0 else (y, 1, 0))
         if h == 0:
             for copy in schur_in[1]:
                 copy.wait()
@@ -361,13 +419,12 @@
         alpha = rz_now[h] / curve
         for c in range(2):
             for rows, value in summed(s, 2, h, c):
-                value = r[h, c, rows, :] - alpha * value
-                r[h, c, rows, :] = value
+                value = r2[h, c, rows, :] - alpha * value
+                r2[h, c, rows, :] = value
                 operand(c, rows, value)
-                x[h, c, rows, :] = alpha * d[h, c, rows, :]
+                x2[h, c, rows, :] = alpha * d[h, c, rows, :]
         sent(y, 1, h)
-        part = precondition(1, h, (lambda: send(s, 2, 1, TAIL)) if h == 0 else (lambda: send(y, 3, 0, TAIL)))
-        send(y, 3, h, HEAD)
+        part = precondition(1, h, 3, (s, 2, 1) if h == 0 else (y, 3, 0))
         reduce_begin(2 + h, part, zero)
         reduce_middle(2 + h)
     send(y, 3, 1, TAIL)
@@ -389,19 +446,19 @@
         reduce_middle(4 + h)
         send(s, 4, h, TAIL)
 
-    sol_copy = [pltpu.make_async_copy(x.at[h], sol_out.at[h], out_sem.at[h]) for h in range(2)]
-    res_copy = [pltpu.make_async_copy(r.at[h], res_out.at[h], out_sem.at[2 + h]) for h in range(2)]
+    sol_copy = [pltpu.make_async_copy(x.at[h], sol_out.at[0, :, :, :, pl.ds(h * HALF, HALF)], out_sem.at[h]) for h in range(2)]
+    res_copy = [pltpu.make_async_copy(r.at[h], res_out.at[0, :, :, :, pl.ds(h * HALF, HALF)], out_sem.at[2 + h]) for h in range(2)]
     for h in range(2):
         sent(ld, 0, h)
         curve, _ = reduce_end(4 + h)
         alpha = rz_new[h] / curve
         for c in range(2):
-            x[h, c] = x[h, c] + alpha * d[h, c]
+            x2[h, c] = x2[h, c] + alpha * d[h, c]
         sol_copy[h].start()
         receive(s, 4, h)
         for c in range(2):
             for rows, value in summed(s, 4, h, c):
-                r[h, c, rows, :] = r[h, c, rows, :] - alpha * value
+                r2[h, c, rows, :] = r2[h, c, rows, :] - alpha * value
         res_copy[h].start()
     for h in range(2):
         sent(y, 3, h)
@@ -410,17 +467,25 @@
         res_copy[h].wait()
 
 
-def place(roles, sol_in, res_in, sol_out, res_out):
-    for h in range(2):
-        sol_out[0, 0, :, h * HALF : (h + 1) * HALF] = sol_in[h, 0]
-        res_out[0, 0, :, h * HALF : (h + 1) * HALF] = res_in[h, 0]
+def place(roles, sol_in, res_in, sol_out, res_out, sem):
+    copies = []
+    for c in range(2):
+        for i in range(NB):
+            to = roles[0, c, role_at(i)]
+            for n, (src, dst) in enumerate(((sol_in, sol_out), (res_in, res_out))):
+                copies.append(pltpu.make_async_copy(src.at[0, c, i], dst.at[0, c, to], sem.at[n, c, i]))
+    for copy in copies:
+        copy.start()
+    for copy in copies:
+        copy.wait()
 
 
 def body(loads, schur, local_inv, basis, coarse_inv, primal, block_roles):
     vec = pltpu.VMEM((2, 2, NI, HALF), F32)
+    blocks = pltpu.VMEM((2, 2, NB, BLOCK, HALF), F32)
     dma = pltpu.SemaphoreType.DMA
     any_space = pl.BlockSpec(memory_space=pl.ANY)
-    half = jax.ShapeDtypeStruct((2, 2, NI, HALF), F32)
+    half = jax.ShapeDtypeStruct((1, 2, NB, BLOCK, 2 * HALF), F32)
     sol, res = pl.pallas_call(
         kernel,
         out_shape=(half, half),
@@ -428,7 +493,7 @@
         out_specs=(any_space, any_space),
         scratch_shapes=[
             pltpu.VMEM((2, NB, BLOCK, HALF), F32), pltpu.VMEM((2, NB, BLOCK, HALF), F32),
-            vec, vec, vec, vec, vec, vec,
+            vec, blocks, vec, vec, vec, blocks,
             pltpu.VMEM((5, 2, 2, 2, 384, HALF), F32),
             pltpu.VMEM((NB, NB, BLOCK, BLOCK), F32), pltpu.VMEM((NB, NB, BLOCK, BLOCK), F32),
             pltpu.VMEM((4, NI, NI), BF16),
@@ -447,11 +512,12 @@
             pltpu.VMEM((2, 2, 4, 2, HALF, HALF), F32),
             pltpu.VMEM((6, 8, 2, HALF), F32),
             pltpu.VMEM((6, 16, 2, HALF), F32),
+            pltpu.VMEM((6, 2, HALF), F32),
             dma((2,)), dma((4, NB)), dma((NB,)), dma, dma((4,)),
             dma((5, 2, 8)), dma((5, 2, 8)),
             dma((3,)), dma((3,)),
             dma((2, 2, 3)), dma((2, 2, 3)),
-            dma((6, 8)), dma((6, 8)), dma((6, 16)), dma((6, 16)),
+            dma((6, 8)), dma((6, 8)), dma((6, 16)), dma((6, 16)), dma((6,)), dma((6,)),
         ],
         compiler_params=pltpu.CompilerParams(
             collective_id=0, has_side_effects=True, vmem_limit_bytes=62 * 2**20
@@ -465,16 +531,14 @@
         basis,
         coarse_inv,
     )
-    out = jax.ShapeDtypeStruct(loads.shape, F32)
-    held = pl.BlockSpec((2, 1, BLOCK, HALF), lambda c, i, roles: (0, c, i, 0))
-    given = pl.BlockSpec((1, 1, BLOCK, 2 * HALF), lambda c, i, roles: (0, c, roles[0, c, role_at(i)], 0))
-    return pl.pallas_call(
+    sol, res = pl.pallas_call(
         place,
-        out_shape=(out, out),
-        grid_spec=pltpu.PrefetchScalarGridSpec(
-            num_scalar_prefetch=1, grid=(2, NB), in_specs=[held, held], out_specs=(given, given)
-        ),
+        out_shape=(half, half),
+        in_specs=[pl.BlockSpec(memory_space=pltpu.SMEM)] + [pl.BlockSpec(memory_space=pltpu.VMEM)] * 2,
+        out_specs=(any_space, any_space),
+        scratch_shapes=[dma((2, 2, NB))],
     )(block_roles, sol, res)
+    return sol.reshape(loads.shape), res.reshape(loads.shape)
 
 
 def solution(mesh):

time: 171 us -> 143 us (0.84)
  the two profiles are of different devices: /device:TPU:1 before, /device:TPU:6 now
where the time goes in v2:
time: 143 us
  Pallas kernels  142 us (99%)
    pallas_call x1, Pallas kernels, body(): pl.pallas_call(kernel, out_shape=(half, half), in_specs=[pl.BlockSpec(mem...  138 us
    pallas_call x1, Pallas kernels, body(): pl.pallas_call(place, out_shape=(half, half), in_specs=[pl.BlockSpec(memo...  4.5 us

profile of v2, /device:TPU:6, one launch (start us, length us, event | category | flops | bytes accessed | tf_op | source)
XLA Modules:
  0.0 143.1 jit_solution(1154078943036594405)
XLA Ops:
  0.6 137.8 %shard_map.86 = (f32[1,2,8,128,256]{4,3,2,1,0:T(8,128)}, f32[1,2,8,128,256]{4,3,2,1,0:T(8,128)}) custom-call(s32[1,2,8]{2,1,0:T(2,128)} %roles.3, s32[1,2,48]{2,1,0:T(2,128)} %primal.1, f32[1,2,8,128,256]{4,3,2,1,0:T(8,128)} %bitcast.7, f32[1,2,8,128,1024]{4,3,2,1,0:T(8,128)} %bitcast.5, f32[1,2,8,128,1024]{4,3,2,1,0:T(8,128)} %bitcast.6, ...), custom_call_target="tpu_custom_call" | custom-call | tf_op jit(solution)/shard_map/pallas_call | solution.py:489
  138.4 4.5 %shard_map.87 = (f32[1,2,8,128,256]{4,3,2,1,0:T(8,128)}, f32[1,2,8,128,256]{4,3,2,1,0:T(8,128)}) custom-call(s32[1,2,8]{2,1,0:T(2,128)} %roles.3, f32[1,2,8,128,256]{4,3,2,1,0:T(8,128)} %get-tuple-element.6.sol_in, f32[1,2,8,128,256]{4,3,2,1,0:T(8,128)} %get-tuple-element.7.res_in), custom_call_target="tpu_custom_call" | custom-call | tf_op jit(solution)/shard_map/pallas_call | solution.py:534

commit v3 on v2

--- a/solution.py
+++ b/solution.py
@@ -119,24 +119,22 @@
             device_id_type=MESH,
         )
 
-    HEAD = ((0, 0), (0, 1))
-    SOON = ((0, 2), (0, 3))
-    TAIL = SOON + ((1, 0), (1, 1), (1, 2), (1, 3))
+    HEAD = ((0, 2), (0, 3))
+    SOON = ((1, 2), (1, 3))
+    REST = ((0, 0), (0, 1), (1, 0), (1, 1))
+    TAIL = SOON + REST
 
     def send(buf, n, h, which):
         for c, kind in which:
             face(buf, n, h, c, kind).start()
 
     def send_rest(buf, n, h, over_z):
-        for c, kind in TAIL:
+        for c, kind in REST:
             z_way = crossing[KINDS[kind][2]]
-            if (c, kind) in SOON:
-                if not over_z:
-                    face(buf, n, h, c, kind).start()
-            else:
-                @pl.when(z_way if over_z else jnp.logical_not(z_way))
-                def _():
-                    face(buf, n, h, c, kind).start()
+
+            @pl.when(z_way if over_z else jnp.logical_not(z_way))
+            def _():
+                face(buf, n, h, c, kind).start()
 
     def receive(buf, n, h):
         for c, kind in HEAD + TAIL:
@@ -342,13 +340,16 @@
         vs[c, rows, 0:HALF] = hi
         vs[c, rows, HALF:] = lo
 
-    def precondition(m, h, out, waiting):
+    def precondition(m, h, out, waiting, between=None):
         for c in range(2):
             wide = jnp.dot(bh[c], vs[c], preferred_element_type=F32)
             low = jnp.dot(bl[c], vs[c, :, 0:HALF], preferred_element_type=F32)
             rowsall[m, h, col, c, 0:NPRIM, :] = wide[:, 0:HALF] + wide[:, HALF:] + low
         rows_copy(m, h, col, opp, 1).start()
         rows_copy(m, h, col, mate, 0).start()
+        send(*waiting, SOON)
+        if between is not None:
+            reduce_middle(between)
         send_rest(*waiting, False)
         apply(0, h, y, None)
         rows_copy(m, h, opp, col, 1).wait_recv()
@@ -371,7 +372,7 @@
             value = y[h, c, rows, :] + (wide[:, 0:HALF] + wide[:, HALF:] + low)
             y[h, c, rows, :] = value
 
-            @pl.when(index == 1)
+            @pl.when(index == 2)
             def _():
                 send(y, out, h, HEAD)
 
@@ -406,11 +407,11 @@
                 d[h, c, rows, :] = value
                 operand(c, rows, value)
         part = apply(2, h, s, d)
-        send(s, 2, h, HEAD)
+        send(s, 2, h, HEAD if h else HEAD + SOON)
         reduce_begin(h, rz_part[h], part)
         reduce_middle(h)
         if h == 0:
-            send(s, 2, 0, TAIL)
+            send(s, 2, 0, REST)
 
     rz_now = [None, None]
     for h in range(2):
@@ -424,10 +425,9 @@
                 operand(c, rows, value)
                 x2[h, c, rows, :] = alpha * d[h, c, rows, :]
         sent(y, 1, h)
-        part = precondition(1, h, 3, (s, 2, 1) if h == 0 else (y, 3, 0))
+        part = precondition(1, h, 3, (s, 2, 1) if h == 0 else (y, 3, 0), 2 if h else None)
         reduce_begin(2 + h, part, zero)
-        reduce_middle(2 + h)
-    send(y, 3, 1, TAIL)
+    send(y, 3, 1, SOON)
 
     rz_new = [None, None]
     for h in range(2):
@@ -439,12 +439,15 @@
                 value = value + beta * d[h, c, rows, :]
                 d[h, c, rows, :] = value
                 operand(c, rows, value)
+        if h == 0:
+            reduce_middle(3)
+            send(y, 3, 1, REST)
         sent(s, 2, h)
         part = apply(2, h, s, d)
-        send(s, 4, h, HEAD)
+        send(s, 4, h, HEAD + SOON)
         reduce_begin(4 + h, part, zero)
         reduce_middle(4 + h)
-        send(s, 4, h, TAIL)
+        send(s, 4, h, REST)
 
     sol_copy = [pltpu.make_async_copy(x.at[h], sol_out.at[0, :, :, :, pl.ds(h * HALF, HALF)], out_sem.at[h]) for h in range(2)]
     res_copy = [pltpu.make_async_copy(r.at[h], res_out.at[0, :, :, :, pl.ds(h * HALF, HALF)], out_sem.at[2 + h]) for h in range(2)]

time: 143 us -> 131 us (0.916)
  Pallas kernels: 142 us -> 131 us
    pallas_call x1, Pallas kernels: 138 us -> 126 us  [body(): pl.pallas_call(kernel, out_shape=(half, half), in_specs=[pl.BlockSpec(mem...]
where the time goes in v3:
time: 131 us
  Pallas kernels  131 us (100%)
    pallas_call x1, Pallas kernels, body(): pl.pallas_call(kernel, out_shape=(half, half), in_specs=[pl.BlockSpec(mem...  126 us
    pallas_call x1, Pallas kernels, body(): pl.pallas_call(place, out_shape=(half, half), in_specs=[pl.BlockSpec(memo...  4.5 us

profile of v3, /device:TPU:6, one launch (start us, length us, event | category | flops | bytes accessed | tf_op | source)
XLA Modules:
  0.0 131.4 jit_solution(7214335630772938840)
XLA Ops:
  0.6 126.1 %shard_map.86 = (f32[1,2,8,128,256]{4,3,2,1,0:T(8,128)}, f32[1,2,8,128,256]{4,3,2,1,0:T(8,128)}) custom-call(s32[1,2,8]{2,1,0:T(2,128)} %roles.3, s32[1,2,48]{2,1,0:T(2,128)} %primal.1, f32[1,2,8,128,256]{4,3,2,1,0:T(8,128)} %bitcast.7, f32[1,2,8,128,1024]{4,3,2,1,0:T(8,128)} %bitcast.5, f32[1,2,8,128,1024]{4,3,2,1,0:T(8,128)} %bitcast.6, ...), custom_call_target="tpu_custom_call" | custom-call | tf_op jit(solution)/shard_map/pallas_call | solution.py:492
  126.7 4.5 %shard_map.87 = (f32[1,2,8,128,256]{4,3,2,1,0:T(8,128)}, f32[1,2,8,128,256]{4,3,2,1,0:T(8,128)}) custom-call(s32[1,2,8]{2,1,0:T(2,128)} %roles.3, f32[1,2,8,128,256]{4,3,2,1,0:T(8,128)} %get-tuple-element.6.sol_in, f32[1,2,8,128,256]{4,3,2,1,0:T(8,128)} %get-tuple-element.7.res_in), custom_call_target="tpu_custom_call" | custom-call | tf_op jit(solution)/shard_map/pallas_call | solution.py:537

commit v4 on v3

--- a/solution.py
+++ b/solution.py
@@ -120,8 +120,8 @@
         )
 
     HEAD = ((0, 2), (0, 3))
-    SOON = ((1, 2), (1, 3))
-    REST = ((0, 0), (0, 1), (1, 0), (1, 1))
+    SOON = ((1, 2), (1, 3), (0, 0), (0, 1))
+    REST = ((1, 0), (1, 1))
     TAIL = SOON + REST
 
     def send(buf, n, h, which):

time: 131 us -> 177 us (1.35); the launches traced: 131 us -> 176 us
  Pallas kernels: 131 us -> 175 us
    pallas_call x1, Pallas kernels: 126 us -> 170 us  [body(): pl.pallas_call(kernel, out_shape=(half, half), in_specs=[pl.BlockSpec(mem...]
where the time goes in v4:
time: 177 us; the launch traced here: 176 us
  Pallas kernels  175 us (99%)
    pallas_call x1, Pallas kernels, body(): pl.pallas_call(kernel, out_shape=(half, half), in_specs=[pl.BlockSpec(mem...  170 us
    pallas_call x1, Pallas kernels, body(): pl.pallas_call(place, out_shape=(half, half), in_specs=[pl.BlockSpec(memo...  4.5 us

profile of v4, /device:TPU:6, one launch (start us, length us, event | category | flops | bytes accessed | tf_op | source)
XLA Modules:
  0.0 175.5 jit_solution(10659304216468211683)
XLA Ops:
  0.6 170.2 %shard_map.86 = (f32[1,2,8,128,256]{4,3,2,1,0:T(8,128)}, f32[1,2,8,128,256]{4,3,2,1,0:T(8,128)}) custom-call(s32[1,2,8]{2,1,0:T(2,128)} %roles.3, s32[1,2,48]{2,1,0:T(2,128)} %primal.1, f32[1,2,8,128,256]{4,3,2,1,0:T(8,128)} %bitcast.7, f32[1,2,8,128,1024]{4,3,2,1,0:T(8,128)} %bitcast.5, f32[1,2,8,128,1024]{4,3,2,1,0:T(8,128)} %bitcast.6, ...), custom_call_target="tpu_custom_call" | custom-call | tf_op jit(solution)/shard_map/pallas_call | solution.py:492
  170.8 4.5 %shard_map.87 = (f32[1,2,8,128,256]{4,3,2,1,0:T(8,128)}, f32[1,2,8,128,256]{4,3,2,1,0:T(8,128)}) custom-call(s32[1,2,8]{2,1,0:T(2,128)} %roles.3, f32[1,2,8,128,256]{4,3,2,1,0:T(8,128)} %get-tuple-element.6.sol_in, f32[1,2,8,128,256]{4,3,2,1,0:T(8,128)} %get-tuple-element.7.res_in), custom_call_target="tpu_custom_call" | custom-call | tf_op jit(solution)/shard_map/pallas_call | solution.py:537
